TPU v7x, 32 devices: a whole 2x2x4 slice. The times are simulated.
32 devices in a mesh: dp: 8 (over z, y), expert: 4 (over x, core).
Axes of the slice: x: 2, y: 2, z: 4, core: 2. Of those that a mesh axis runs over, the one named last changes fastest.
Arguments:
- tokens: bfloat16 [8192, 7168], P(('dp', 'expert')), may hold values from -6 to 6
- routes: int32 [8192, 8], P(('dp', 'expert')), may hold values from 0 to 255, as said below
- slot_ids: int32 [8192, 8], P(('dp', 'expert')), may hold values from -1 to 15, as said below
- gate_weight: bfloat16 [4, 2048, 7168], P('expert', 'dp'), may hold values from -0.0625 to 0.0625
- up_weight: bfloat16 [4, 2048, 7168], P('expert', 'dp'), may hold values from -0.0625 to 0.0625
Outputs:
- input_hessian: float32 [4, 7168, 7168], P('expert', 'dp')
- down_hessian: float32 [4, 2048, 2048], P('expert', 'dp')
Inputs may be any that keep to these rules, and one draw needn't show every extreme that they name: `routes`: distinct ids in each row. On each device, no window expert is named by more than 16 tokens, and in every group of 4 consecutive devices along dp+expert (one index of dp) some window expert is named by exactly 16 tokens on every one of them. Every window expert is named on every device. `slot_ids`: for a choice of a window expert: on each device, the tokens naming that expert hold the slots 0 to n - 1, each once; for ids of 4 or more the slot is -1.
All inputs are finite; a program needn't handle non-finite values.
Results may differ from a plain program's by a relative error of at most 0.0038.
Values may be sent and summed in bfloat16 or wider, within the bound.
A program may use at most 192 MiB of HBM per device.

v0:
```python
import jax
import jax.numpy as jnp
from jax import lax
from jax.sharding import PartitionSpec as P

CAP = 16


def expert_work(rows_in, gate_rows, up_rows, first_col, col_count):
    columns = lax.dynamic_slice_in_dim(rows_in, first_col, col_count, 1)
    gram = lax.dot_general(
        columns, rows_in, (((0,), (0,)), ((), ())), preferred_element_type=jnp.float32
    )
    gate = lax.dot_general(
        gate_rows, rows_in, (((1,), (1,)), ((), ())), preferred_element_type=jnp.float32
    )
    upward = lax.dot_general(
        up_rows, rows_in, (((1,), (1,)), ((), ())), preferred_element_type=jnp.float32
    )
    hidden_t = (jax.nn.silu(gate) * upward).astype(jnp.bfloat16)
    return (gram, hidden_t)


def local(tokens, routes, slot_ids, gate_weight, up_weight):
    width = tokens.shape[1]
    owners = lax.axis_size("expert")
    data_count = lax.axis_size("dp")
    expert_ids = jnp.arange(owners, dtype=jnp.int32)
    member = jnp.any(routes[:, :, None] == expert_ids[None, None, :], axis=1)
    local_counts = jnp.sum(member.astype(jnp.float32), axis=0)
    totals = lax.psum(local_counts, ("dp", "expert"))
    routed = jnp.take(totals, lax.axis_index("expert"))
    factor = 2.0 / routed
    slot_lanes = jnp.arange(owners * CAP, dtype=jnp.int32)
    matched = (routes[None, :, :] == (slot_lanes // CAP)[:, None, None]) & (
        slot_ids[None, :, :] == (slot_lanes % CAP)[:, None, None]
    )
    one_hot = jnp.any(matched, axis=2).astype(jnp.bfloat16)
    dispatched = jnp.dot(one_hot, tokens, preferred_element_type=jnp.float32).astype(jnp.bfloat16)
    dispatched = dispatched.reshape(owners, CAP, width)
    gate_rows = gate_weight[0]
    up_rows = up_weight[0]
    col_count = width // data_count
    first_col = lax.axis_index("dp") * col_count
    arrived = lax.all_to_all(dispatched, "expert", split_axis=0, concat_axis=1, tiled=True)[0]
    gathered = lax.all_gather(arrived, "dp", axis=0, tiled=True)
    gram, hidden_t = expert_work(gathered, gate_rows, up_rows, first_col, col_count)
    rows_t = lax.all_to_all(hidden_t, "dp", split_axis=1, concat_axis=0, tiled=True)
    down_block = lax.psum_scatter(
        lax.dot_general(
            rows_t, rows_t, (((1,), (1,)), ((), ())), preferred_element_type=jnp.float32
        ),
        "dp",
        scatter_dimension=0,
        tiled=True,
    )
    return ((gram * factor)[None], (down_block * factor)[None])


def solution(mesh):
    in_specs = (
        P(("dp", "expert"), None),
        P(("dp", "expert"), None),
        P(("dp", "expert"), None),
        P("expert", "dp", None),
        P("expert", "dp", None),
    )
    out_specs = (P("expert", "dp", None), P("expert", "dp", None))
    return jax.shard_map(local, mesh=mesh, in_specs=in_specs, out_specs=out_specs, check_vma=False)
```

profile of v0, /device:TPU:0, one launch (start us, length us, event | category | flops | bytes accessed | tf_op | source)
XLA Modules:
  0.0 462.3 jit_solution(5250093902016924482)
XLA Ops:
  7.2 0.0 all-gather.2.cloned.1.call-start
  7.2 1.0 and_reduce_fusion
  8.2 2.8 convolution_convert_fusion
  11.0 17.2 %all_to_all.28 = bf16[4,16,7168]{2,1,0:T(8,128)(2,1)} all-to-all(bf16[4,16,7168]{2,1,0:T(8,128)(2,1)S(1)} %bitcast.42), channel_id=1, replica_groups=mesh['dp'=8,'expert'=4] {'expert'}, dimensions={0} | all-to-all | bytes 1835008 | tf_op jit(solution)/shard_map/all_to_all | solution.py:45
  28.2 0.0 all-gather.2.cloned.1.call-update
  28.2 0.0 reduce-scatter.2.cloned.1.call-start
  28.3 112.9 %all-gather.2.cloned.1.call-done = bf16[512,7168]{1,0:T(8,128)(2,1)} async-done(((bf16[64,7168]{1,0:T(8,128)(2,1)}), bf16[512,7168]{1,0:T(8,128)(2,1)}) %all-gather.2.cloned.1.call-update) | async-done | bytes 7340048 | tf_op jit(solution)/shard_map/all_gather | solution.py:46
  141.1 0.0 copy-start
  141.1 0.0 copy-start.2
  141.1 6.4 %fusion.4 = f32[256,512]{0,1:T(8,128)S(1)} fusion(bf16[512,7168]{1,0:T(8,128)(2,1)} %all-gather.2.cloned.1.call-done, bf16[1,256,7168]{2,1,0:T(8,128)(2,1)} %param.8), kind=kOutput, calls=%fused_computation.7 | convolution fusion | flops 1879048192 | bytes 11534336 | tf_op jit(solution)/shard_map/dot_general | solution.py:14
  147.5 0.0 copy-done
  147.5 0.9 copy-done.2
  148.4 2.1 fusion.13
  150.5 11.6 %all_to_all.29 = bf16[256,8,64]{0,2,1:T(8,128)(2,1)S(1)} all-to-all(bf16[256,8,64]{0,2,1:T(8,128)(2,1)S(1)} %bitcast.45), channel_id=1, replica_groups=mesh['dp'=8,'expert'=4] {'dp'}, dimensions={1} | all-to-all | bytes 524288 | tf_op jit(solution)/shard_map/all_to_all | solution.py:48
  162.1 8.1 %fusion.19 = f32[2048,2048]{1,0:T(8,128)} fusion(bf16[2048,64]{0,1:T(8,128)(2,1)S(1)} %bitcast.43), kind=kOutput, calls=%fused_computation.22 | convolution fusion | flops 536870912 | bytes 17039360 | tf_op jit(solution)/shard_map/dot_general | solution.py:50
  170.2 0.0 copy-start.1
  170.2 0.0 reduce-scatter.2.cloned.1.call-update
  170.2 0.7 copy-done.1
  170.9 0.1 convert_reduce_fusion
  171.0 42.5 %psum.7 = f32[4]{0:T(128)S(1)} all-reduce(f32[4]{0:T(128)S(1)} %convert_reduce_fusion), channel_id=1, replica_groups=mesh['dp'=8,'expert'=4] {'dp','expert'}, use_global_device_ids=true, to_apply=%region_3.4 | all-reduce | flops 4 | bytes 32 | tf_op jit(solution)/shard_map/psum | solution.py:31
  213.5 0.6 dynamic-slice.2
  214.8 15.2 %multiply_bitcast_fusion = f32[1,896,7168]{2,1,0:T(8,128)} fusion(bf16[512,7168]{1,0:T(8,128)(2,1)} %all-gather.2.cloned.1.call-done, f32[]{:T(128)} %bitcast.3, s32[]{:T(128)S(6)} %select_n.33), kind=kOutput, calls=%fused_computation | convolution fusion | flops 6583091200 | bytes 33948164 | tf_op jit(solution)/shard_map/dot_general | solution.py:11
  230.0 222.4 %reduce-scatter.2.cloned.1.call-done = f32[256,2048]{1,0:T(8,128)} async-done(((f32[2048,2048]{1,0:T(8,128)}), f32[256,2048]{1,0:T(8,128)}) %reduce-scatter.2.cloned.1.call-update) | async-done | bytes 2097168 | tf_op jit(solution)/shard_map/reduce_scatter | solution.py:49
  452.4 3.1 multiply_bitcast_fusion.1
  (3 shorter events, 0.0 us)
Async XLA Ops:
  7.2 134.0 %all-gather.2.cloned.1.call-start = ((), (), s32[]{:S(2)}) async-start(), calls=%async_computation.3 | async-start | bytes 8257536 | tf_op jit(solution)/shard_map/all_gather | solution.py:46
  28.2 424.2 %reduce-scatter.2.cloned.1.call-start = ((), (), s32[]{:S(2)}) async-start(), calls=%async_computation.4 | async-start | bytes 18874368 | tf_op jit(solution)/shard_map/reduce_scatter | solution.py:49
  141.1 6.4 %copy-start = (bf16[512,7168]{1,0:T(8,128)(2,1)S(1)}, bf16[512,7168]{1,0:T(8,128)(2,1)}, u32[]{:S(2)}) copy-start(bf16[512,7168]{1,0:T(8,128)(2,1)} %all-gather.2.cloned.1.call-done) | copy-start | bytes 22020100
  141.1 7.3 %copy-start.2 = (bf16[1,256,7168]{2,1,0:T(8,128)(2,1)S(1)}, bf16[1,256,7168]{2,1,0:T(8,128)(2,1)}, u32[]{:S(2)}) copy-start(bf16[1,256,7168]{2,1,0:T(8,128)(2,1)} %param.9) | copy-start | bytes 11010052
  170.2 0.7 copy-start.1
Sparse Core Ops, SparseCore 0:
  28.3 112.7 all-gather.1
  170.3 281.9 reduce-scatter.1
where the time goes:
time: 463 us; the launch traced here: 462 us
  waiting for transfers between devices  335 us (72%)
  blocking collectives  71.2 us (15%)
  matrix products  34.5 us (7%)
  between operations  14.8 us (3%)
    reduce_scatter x1, waiting for transfers between devices, local(): lax.psum_scatter(lax.dot_general(rows_t, rows_t, (((1,), (1,)), ((), ()))...  222 us
    all_gather x1, waiting for transfers between devices, local(): gathered = lax.all_gather(arrived, 'dp', axis=0, tiled=True)  113 us
    psum x1, blocking collectives, local(): totals = lax.psum(local_counts, ('dp', 'expert'))  42.5 us
    all_to_all x1, blocking collectives, local(): lax.all_to_all(dispatched, 'expert', split_axis=0, concat_axis=1, tiled=T...  17.2 us
    dot_general x1, matrix products, expert_work(): lax.dot_general(columns, rows_in, (((0,), (0,)), ((), ())), preferred_ele...  15.2 us
    all_to_all x1, blocking collectives, local(): lax.all_to_all(hidden_t, 'dp', split_axis=1, concat_axis=0, tiled=True)  11.6 us
  transfers between devices with their start and end apart: 2, of which 2 were waited for; matrix products, arithmetic and copies ran while one was open for 3% of the time, Pallas kernels for 0%

commit v1 on v0

v1 whole, which is shorter than its diff:
```python
import functools

import jax
import jax.numpy as jnp
from jax import lax
from jax.experimental import pallas as pl
from jax.experimental.pallas import tpu as pltpu
from jax.sharding import PartitionSpec as P

CAP = 16
MESH = pl.DeviceIdType.MESH


def peer(e, k, owners):
    return ((e // 2 + k // 2) % (owners // 2)) * 2 + (e + k) % 2


def gather_kernel(n, owners, hot_ref, tok_ref, gate_ref, up_ref, x_ref, hid_ref,
                  xbuf, sbuf, wg, wu, acc_g, acc_u,
                  w_sem, out_sem, ex_send, ex_recv, ring_send, ring_recv):
    width = tok_ref.shape[1]
    block = owners * CAP
    half = n // 2
    me, e = lax.axis_index("dp"), lax.axis_index("expert")

    odd = me % 2
    pos = (1 - odd) * (me // 2) + odd * (n - 1 - me // 2)

    def at(p):
        late = p // half
        return (1 - late) * (2 * p) + late * (2 * (n - 1 - p) + 1)

    near = (at((pos + 1) % n), at((pos + n - 1) % n))

    barrier = pltpu.get_barrier_semaphore()
    for k in range(1, owners):
        pl.semaphore_signal(barrier, inc=1, device_id=(me, peer(e, k, owners)), device_id_type=MESH)
    for other in near:
        pl.semaphore_signal(barrier, inc=1, device_id=(other, e), device_id_type=MESH)

    loads = [
        pltpu.make_async_copy(gate_ref, wg, w_sem.at[0]),
        pltpu.make_async_copy(up_ref, wu, w_sem.at[1]),
    ]
    for load in loads:
        load.start()

    step_cols = 1024 if width % 1024 == 0 else 128

    def dispatch(j, carry):
        cols = pl.ds(pl.multiple_of(j * step_cols, step_cols), step_cols)
        rows = jnp.dot(hot_ref[...], tok_ref[:, cols], preferred_element_type=jnp.float32)
        rows = rows.astype(jnp.bfloat16)
        xbuf[0:CAP, cols] = rows[0:CAP]
        sbuf[:, cols] = rows[CAP:]
        return carry

    lax.fori_loop(0, width // step_cols, dispatch, 0)
    pl.semaphore_wait(barrier, owners + 1)

    pending = []
    arrive = {}
    for k in range(1, owners):
        copy = pltpu.make_async_remote_copy(
            src_ref=sbuf.at[pl.ds((k - 1) * CAP, CAP)],
            dst_ref=xbuf.at[pl.ds(k * CAP, CAP)],
            send_sem=ex_send.at[k],
            recv_sem=ex_recv.at[k],
            device_id=(me, peer(e, k, owners)),
            device_id_type=MESH,
        )
        copy.start()
        pending.append(copy)
        arrive[(0, 0, k)] = copy

    def slot(d, s):
        if s == 0:
            return 0
        return n - 1 if s == half else 2 * s - 1 + d

    def forward(d, s, c):
        copy = pltpu.make_async_remote_copy(
            src_ref=xbuf.at[pl.ds(slot(d, s - 1) * block + c * CAP, CAP)],
            dst_ref=xbuf.at[pl.ds(slot(d, s) * block + c * CAP, CAP)],
            send_sem=ring_send.at[d, s, c],
            recv_sem=ring_recv.at[d, s, c],
            device_id=(near[d], e),
            device_id_type=MESH,
        )
        copy.start()
        pending.append(copy)
        arrive[(d, s, c)] = copy

    def hidden(first, count, places):
        rows = count * block
        base = first * block
        acc_g[0:rows, :] = jnp.zeros((rows, acc_g.shape[1]), jnp.float32)
        acc_u[0:rows, :] = jnp.zeros((rows, acc_u.shape[1]), jnp.float32)

        def body(j, carry):
            cols = pl.ds(pl.multiple_of(j * step_cols, step_cols), step_cols)
            part = xbuf[base:base + rows, cols]
            dims = (((1,), (1,)), ((), ()))
            acc_g[0:rows, :] += lax.dot_general(part, wg[:, cols], dims, preferred_element_type=jnp.float32)
            acc_u[0:rows, :] += lax.dot_general(part, wu[:, cols], dims, preferred_element_type=jnp.float32)
            return carry

        lax.fori_loop(0, width // step_cols, body, 0)
        gate = acc_g[0:rows, :]
        out = (gate / (1.0 + jnp.exp(-gate)) * acc_u[0:rows, :]).astype(jnp.bfloat16)
        for i, place in enumerate(places):
            hid_ref[pl.ds(pl.multiple_of(place * block, block), block), :] = out[i * block:(i + 1) * block]

    stores = []

    def keep(first, count):
        rows = pl.ds(first * block, count * block)
        copy = pltpu.make_async_copy(xbuf.at[rows], x_ref.at[rows], out_sem.at[first])
        copy.start()
        stores.append(copy)

    for s in range(1, half + 1):
        for c in range(owners):
            if s == 1:
                if c > 0:
                    arrive[(0, 0, c)].wait_recv()
            else:
                arrive[(0, s - 1, c)].wait_recv()
                arrive[(1, s - 1, c)].wait_recv()
            if s < half:
                forward(0, s, c)
                forward(1, s, c)
            else:
                forward(0 if c < owners // 2 else 1, s, c)
        if s == 1:
            keep(0, 1)
            for load in loads:
                load.wait()
            hidden(0, 1, [pos])
        else:
            first = slot(0, s - 1)
            keep(first, 2)
            hidden(first, 2, [(pos + n - (s - 1)) % n, (pos + s - 1) % n])
    for c in range(owners):
        arrive[(0 if c < owners // 2 else 1, half, c)].wait_recv()
    keep(n - 1, 1)
    hidden(n - 1, 1, [(pos + half) % n])
    for copy in pending:
        copy.wait_send()
    for copy in stores:
        copy.wait()


def gather(hot, tokens, gate_rows, up_rows, n, owners):
    width = tokens.shape[1]
    units = gate_rows.shape[0]
    block = owners * CAP
    half = n // 2
    vmem = pl.BlockSpec(memory_space=pltpu.VMEM)
    hbm = pl.BlockSpec(memory_space=pl.ANY)
    rows = n * block
    return pl.pallas_call(
        functools.partial(gather_kernel, n, owners),
        out_shape=(
            jax.ShapeDtypeStruct((rows, width), jnp.bfloat16),
            jax.ShapeDtypeStruct((rows, units), jnp.bfloat16),
        ),
        in_specs=[vmem, vmem, hbm, hbm],
        out_specs=(hbm, vmem),
        scratch_shapes=[
            pltpu.VMEM((rows, width), jnp.bfloat16),
            pltpu.VMEM((block - CAP, width), jnp.bfloat16),
            pltpu.VMEM((units, width), jnp.bfloat16),
            pltpu.VMEM((units, width), jnp.bfloat16),
            pltpu.VMEM((2 * block, units), jnp.float32),
            pltpu.VMEM((2 * block, units), jnp.float32),
            pltpu.SemaphoreType.DMA((2,)),
            pltpu.SemaphoreType.DMA((n,)),
            pltpu.SemaphoreType.DMA((owners,)),
            pltpu.SemaphoreType.DMA((owners,)),
            pltpu.SemaphoreType.DMA((2, half + 1, owners)),
            pltpu.SemaphoreType.DMA((2, half + 1, owners)),
        ],
        compiler_params=pltpu.CompilerParams(
            collective_id=0, has_side_effects=True, vmem_limit_bytes=56 * 1024 * 1024
        ),
        cost_estimate=pl.CostEstimate(
            flops=4 * rows * width * units, bytes_accessed=6 * rows * width, transcendentals=rows * units
        ),
    )(hot, tokens, gate_rows, up_rows)


def local(tokens, routes, slot_ids, gate_weight, up_weight):
    width = tokens.shape[1]
    owners = lax.axis_size("expert")
    data_count = lax.axis_size("dp")
    e = lax.axis_index("expert")
    expert_ids = jnp.arange(owners, dtype=jnp.int32)
    member = jnp.any(routes[:, :, None] == expert_ids[None, None, :], axis=1)
    local_counts = jnp.sum(member.astype(jnp.float32), axis=0)
    totals = lax.psum(local_counts, ("dp", "expert"))
    routed = jnp.take(totals, e)
    factor = 2.0 / routed

    lanes = jnp.arange(owners * CAP, dtype=jnp.int32)
    wanted = peer(e, lanes // CAP, owners)
    matched = (routes[None, :, :] == wanted[:, None, None]) & (
        slot_ids[None, :, :] == (lanes % CAP)[:, None, None]
    )
    one_hot = jnp.any(matched, axis=2).astype(jnp.bfloat16)
    rows, hidden = gather(one_hot, tokens, gate_weight[0], up_weight[0], data_count, owners)
    col_count = width // data_count
    first_col = lax.axis_index("dp") * col_count
    hidden_all = lax.all_gather(hidden, "dp", axis=0, tiled=False)
    columns = lax.dynamic_slice_in_dim(rows, first_col, col_count, 1)
    gram = lax.dot_general(
        columns, rows, (((0,), (0,)), ((), ())), preferred_element_type=jnp.float32
    )
    down = lax.dot_general(
        hidden, hidden_all, (((0,), (1,)), ((), ())), preferred_element_type=jnp.float32
    )
    down = down.reshape(down.shape[0], -1)
    return ((gram * factor)[None], (down * factor)[None])


def solution(mesh):
    in_specs = (
        P(("dp", "expert"), None),
        P(("dp", "expert"), None),
        P(("dp", "expert"), None),
        P("expert", "dp", None),
        P("expert", "dp", None),
    )
    out_specs = (P("expert", "dp", None), P("expert", "dp", None))
    return jax.shard_map(local, mesh=mesh, in_specs=in_specs, out_specs=out_specs, check_vma=False)
```

time: 463 us -> 159 us (0.34)
  waiting for transfers between devices: 335 us -> 0.02 us
  Pallas kernels: 0 us -> 81.2 us
  blocking collectives: 71.2 us -> 41.3 us
  matrix products: 34.5 us -> 17.5 us
    reduce_scatter x1 -> x0, waiting for transfers between devices: 222 us -> none  [local(): lax.psum_scatter(lax.dot_general(rows_t, rows_t, (((1,), (1,)), ((), ()))...]
    all_gather x1, waiting for transfers between devices: 113 us -> 0.01 us  [local(): hidden_all = lax.all_gather(hidden, 'dp', axis=0, tiled=False)]
    pallas_call x0 -> x1, Pallas kernels: none -> 81.2 us  [gather(): pl.pallas_call(functools.partial(gather_kernel, n, owners), out_shape=(ja...]
    all_to_all x2 -> x0, blocking collectives: 28.8 us -> none  [the longest x1 17.2 us: local(): lax.all_to_all(dispatched, 'expert', split_axis=0, concat_axis=1, tiled=T...]
    dot_general x5 -> x2, matrix products: 34.5 us -> 17.5 us  [the longest x1 15 us: local(): lax.dot_general(columns, rows, (((0,), (0,)), ((), ())), preferred_elemen...]
  transfers between devices with their start and end apart: 2 -> 1, of which waited for: 2 -> 0; matrix products, arithmetic and copies ran while one was open for 3% -> 10% of each run, Pallas kernels for 0% -> 0%
where the time goes in v1:
time: 159 us
  Pallas kernels  81.2 us (51%)
  blocking collectives  41.3 us (26%)
  matrix products  17.5 us (11%)
  between operations  14.8 us (9%)
  local copies, waits for them, and re-layouts  2.41 us (2%)
  other arithmetic  1.77 us (1%)
    pallas_call x1, Pallas kernels, gather(): pl.pallas_call(functools.partial(gather_kernel, n, owners), out_shape=(ja...  81.2 us
    psum x1, blocking collectives, local(): totals = lax.psum(local_counts, ('dp', 'expert'))  41.3 us
    dot_general x1, matrix products, local(): lax.dot_general(columns, rows, (((0,), (0,)), ((), ())), preferred_elemen...  15 us
  transfers between devices with their start and end apart: 1, of which 0 were waited for; matrix products, arithmetic and copies ran while one was open for 10% of the time, Pallas kernels for 0%

profile of v1, /device:TPU:0, one launch (start us, length us, event | category | flops | bytes accessed | tf_op | source)
XLA Modules:
  0.0 159.0 jit_solution(3263046088580762478)
XLA Ops:
  7.2 0.0 all-gather.3.cloned.1.call-start
  7.2 1.0 and_reduce_fusion
  8.2 0.6 convert_element_type.6.hot_ref
  8.9 0.0 copy-start.1
  8.9 81.2 %shard_map.68 = (bf16[512,7168]{1,0:T(8,128)(2,1)}, bf16[512,256]{1,0:T(8,128)(2,1)}) custom-call(bf16[64,256]{1,0:T(8,128)(2,1)} %convert_element_type.6.hot_ref, bf16[256,7168]{1,0:T(8,128)(2,1)} %tok_ref.1, bf16[256,7168]{1,0:T(8,128)(2,1)} %bitcast.15, bf16[256,7168]{1,0:T(8,128)(2,1)} %bitcast.16), custom_call_target="tpu_custom_call" | custom-call | flops 3758096384 | bytes 22020096 | tf_op jit(solution)/shard_map/pallas_call | solution.py:162
  90.1 0.0 all-gather.3.cloned.1.call-update
  90.1 0.0 copy-done.1
  90.1 0.1 convert_reduce_fusion
  90.2 41.3 %psum.7 = f32[4]{0:T(128)S(1)} all-reduce(f32[4]{0:T(128)S(1)} %convert_reduce_fusion), channel_id=1, replica_groups=mesh['dp'=8,'expert'=4] {'dp','expert'}, use_global_device_ids=true, to_apply=%region_3.4 | all-reduce | flops 4 | bytes 32 | tf_op jit(solution)/shard_map/psum | solution.py:201
  131.5 0.6 dynamic-slice.2
  132.8 0.0 copy-start
  132.8 15.0 %multiply_bitcast_fusion = f32[1,896,7168]{2,1,0:T(8,128)} fusion(bf16[512,7168]{1,0:T(8,128)(2,1)} %get-tuple-element.4, f32[]{:T(128)} %bitcast.3, s32[]{:T(128)S(6)} %select_n.66), kind=kOutput, calls=%fused_computation | convolution fusion | flops 6583091200 | bytes 33948164 | tf_op jit(solution)/shard_map/dot_general | solution.py:216
  147.8 0.0 all-gather.3.cloned.1.call-done
  147.8 0.0 copy-done
  147.8 2.5 %convolution_multiply_fusion = f32[256,8,256]{0,2,1:T(8,128)S(1)} fusion(bf16[8,512,256]{2,1,0:T(8,128)(2,1)} %bitcast.14, f32[]{:T(128)} %bitcast.3, bf16[512,256]{1,0:T(8,128)(2,1)S(1)} %copy-done), kind=kOutput, calls=%fused_computation.1 | convolution fusion | flops 537395200 | bytes 4456452 | tf_op jit(solution)/shard_map/dot_general | solution.py:219
  150.3 1.8 %copy.13 = f32[1,256,2048]{2,1,0:T(8,128)} copy(f32[1,256,2048]{1,2,0:T(8,128)S(1)} %bitcast.13) | data formatting | bytes 4194304
  (2 shorter events, 0.0 us)
Async XLA Ops:
  7.2 140.7 %all-gather.3.cloned.1.call-start = ((), (), s32[]{:S(2)}) async-start(), calls=%async_computation | async-start | bytes 2359296 | tf_op jit(solution)/shard_map/all_gather | solution.py:214
  8.9 81.2 %copy-start.1 = (s32[256,8]{0,1:T(8,128)S(1)}, s32[256,8]{0,1:T(8,128)}, u32[]{:S(2)}) copy-start(s32[256,8]{0,1:T(8,128)} %param.6) | copy-start | bytes 24580
  132.8 15.0 %copy-start = (bf16[512,256]{1,0:T(8,128)(2,1)S(1)}, bf16[512,256]{1,0:T(8,128)(2,1)}, u32[]{:S(2)}) copy-start(bf16[512,256]{1,0:T(8,128)(2,1)} %get-tuple-element.5) | copy-start | bytes 786436
Sparse Core Ops, SparseCore 0:
  90.2 50.3 all-gather.2

commit v2 on v1

v2 whole, which is shorter than its diff:
```python
import functools

import jax
import jax.numpy as jnp
from jax import lax
from jax.experimental import pallas as pl
from jax.experimental.pallas import tpu as pltpu
from jax.sharding import PartitionSpec as P

CAP = 16
MESH = pl.DeviceIdType.MESH


def peer(e, k, owners):
    return ((e // 2 + k // 2) % (owners // 2)) * 2 + (e + k) % 2


def gather_kernel(n, owners, route_ref, slot_ref, tok_ref, gate_ref, up_ref, x_ref, down_ref, factor_ref,
                  xbuf, sbuf, wg, wu, acc_g, acc_u, hbuf, mine, counts, held_counts,
                  w_sem, out_sem, ex_send, ex_recv, cx_send, cx_recv,
                  ring_send, ring_recv, hid_send, hid_recv, cnt_send, cnt_recv):
    width = tok_ref.shape[1]
    block = owners * CAP
    half = n // 2
    me, e = lax.axis_index("dp"), lax.axis_index("expert")

    odd = me % 2
    pos = (1 - odd) * (me // 2) + odd * (n - 1 - me // 2)

    def at(p):
        late = p // half
        return (1 - late) * (2 * p) + late * (2 * (n - 1 - p) + 1)

    near = (at((pos + 1) % n), at((pos + n - 1) % n))

    barrier = pltpu.get_barrier_semaphore()
    for k in range(1, owners):
        pl.semaphore_signal(barrier, inc=1, device_id=(me, peer(e, k, owners)), device_id_type=MESH)
    for other in near:
        pl.semaphore_signal(barrier, inc=1, device_id=(other, e), device_id_type=MESH)

    loads = [
        pltpu.make_async_copy(gate_ref, wg, w_sem.at[0]),
        pltpu.make_async_copy(up_ref, wu, w_sem.at[1]),
    ]
    for load in loads:
        load.start()

    slot_rows = lax.broadcasted_iota(jnp.int32, (CAP, tok_ref.shape[0]), 0)
    picks = []
    for k in range(owners):
        wanted = peer(e, k, owners)
        pick = jnp.zeros(slot_rows.shape, jnp.float32)
        for i in range(route_ref.shape[0]):
            hit = (route_ref[i:i + 1, :] == wanted) & (slot_ref[i:i + 1, :] == slot_rows)
            pick = jnp.where(hit, 1.0, pick)
        picks.append(pick)
        counts[k] = jnp.broadcast_to(jnp.sum(pick, axis=(0, 1), keepdims=True), counts.shape[1:])
    hot = jnp.concatenate(picks, axis=0).astype(jnp.bfloat16)

    step_cols = 1024 if width % 1024 == 0 else 128

    def dispatch(j, carry):
        cols = pl.ds(pl.multiple_of(j * step_cols, step_cols), step_cols)
        rows = jnp.dot(hot, tok_ref[:, cols], preferred_element_type=jnp.float32)
        rows = rows.astype(jnp.bfloat16)
        xbuf[0:CAP, cols] = rows[0:CAP]
        sbuf[:, cols] = rows[CAP:]
        return carry

    lax.fori_loop(0, width // step_cols, dispatch, 0)
    pl.semaphore_wait(barrier, owners + 1)

    pending = []
    arrive = {}

    def send(key, src, dst, send_sem, recv_sem, target):
        copy = pltpu.make_async_remote_copy(
            src_ref=src, dst_ref=dst, send_sem=send_sem, recv_sem=recv_sem,
            device_id=target, device_id_type=MESH,
        )
        copy.start()
        pending.append(copy)
        arrive[key] = copy

    for k in range(1, owners):
        other = (me, peer(e, k, owners))
        send(("x", 0, 0, k), sbuf.at[pl.ds((k - 1) * CAP, CAP)], xbuf.at[pl.ds(k * CAP, CAP)],
             ex_send.at[k], ex_recv.at[k], other)
    for k in range(1, owners):
        other = (me, peer(e, k, owners))
        send(("c", 0, k), counts.at[k], held_counts.at[k], cx_send.at[k], cx_recv.at[k], other)

    def slot(d, s):
        if s == 0:
            return 0
        return n - 1 if s == half else 2 * s - 1 + d

    offsets = [0] * n
    for s in range(1, half):
        offsets[slot(0, s)] = n - s
        offsets[slot(1, s)] = s
    offsets[n - 1] = half
    slot_of = [offsets.index(o) for o in range(n)]

    def forward(d, s, c):
        send(("x", d, s, c),
             xbuf.at[pl.ds(slot(d, s - 1) * block + c * CAP, CAP)],
             xbuf.at[pl.ds(slot(d, s) * block + c * CAP, CAP)],
             ring_send.at[d, s, c], ring_recv.at[d, s, c], (near[d], e))

    ends = sorted({max(1, half * (i + 1) // 4) for i in range(4)})
    bounds = [0] + [n if s == half else 2 * s + 1 for s in ends]
    groups = len(bounds) - 1

    def forward_hidden(d, s, g):
        rows = pl.ds(bounds[g] * block, (bounds[g + 1] - bounds[g]) * block)
        send(("h", d, s, g), hbuf.at[slot(d, s - 1), rows], hbuf.at[slot(d, s), rows],
             hid_send.at[d, s, g], hid_recv.at[d, s, g], (near[d], e))

    def ways(s, g):
        return (0, 1) if s < half else (g % 2,)

    def forward_counts(d, s):
        send(("n", d, s), counts.at[owners + slot(d, s - 1)], counts.at[owners + slot(d, s)],
             cnt_send.at[d, s], cnt_recv.at[d, s], (near[d], e))

    def hidden(first, count):
        rows = count * block
        base = first * block
        acc_g[0:rows, :] = jnp.zeros((rows, acc_g.shape[1]), jnp.float32)
        acc_u[0:rows, :] = jnp.zeros((rows, acc_u.shape[1]), jnp.float32)

        def body(j, carry):
            cols = pl.ds(pl.multiple_of(j * step_cols, step_cols), step_cols)
            part = xbuf[base:base + rows, cols]
            dims = (((1,), (1,)), ((), ()))
            acc_g[0:rows, :] += lax.dot_general(part, wg[:, cols], dims, preferred_element_type=jnp.float32)
            acc_u[0:rows, :] += lax.dot_general(part, wu[:, cols], dims, preferred_element_type=jnp.float32)
            return carry

        lax.fori_loop(0, width // step_cols, body, 0)
        gate = acc_g[0:rows, :]
        out = (gate / (1.0 + jnp.exp(-gate)) * acc_u[0:rows, :]).astype(jnp.bfloat16)
        hbuf[0, base:base + rows, :] = out

    def down(d, s):
        j = slot(d, s)
        for r in range(n):
            own = slot_of[(offsets[j] + offsets[r]) % n]
            mine[r * block:(r + 1) * block, :] = hbuf[0, own * block:(own + 1) * block, :]
        down_ref[at((pos + offsets[j]) % n)] = lax.dot_general(
            mine[...], hbuf[j], (((0,), (0,)), ((), ())), preferred_element_type=jnp.float32
        )

    stores = []

    def keep(first, count):
        rows = pl.ds(first * block, count * block)
        copy = pltpu.make_async_copy(xbuf.at[rows], x_ref.at[rows], out_sem.at[first])
        copy.start()
        stores.append(copy)

    for s in range(1, half + 1):
        for c in range(owners):
            if s == 1:
                if c > 0:
                    arrive[("x", 0, 0, c)].wait_recv()
            else:
                arrive[("x", 0, s - 1, c)].wait_recv()
                arrive[("x", 1, s - 1, c)].wait_recv()
            if s < half:
                forward(0, s, c)
                forward(1, s, c)
            else:
                forward(0 if c < owners // 2 else 1, s, c)
        if s == 1:
            total = counts[0]
            for k in range(1, owners):
                arrive[("c", 0, k)].wait_recv()
                total = total + held_counts[k]
            counts[owners] = total
            forward_counts(0, 1)
            forward_counts(1, 1)
            keep(0, 1)
            for load in loads:
                load.wait()
            hidden(0, 1)
        else:
            arrive[("n", 0, s - 1)].wait_recv()
            arrive[("n", 1, s - 1)].wait_recv()
            forward_counts(0, s)
            if s < half:
                forward_counts(1, s)
            if s == half:
                for g in range(groups - 2):
                    forward_hidden(0, 1, g)
                    forward_hidden(1, 1, g)
            first = slot(0, s - 1)
            keep(first, 2)
            hidden(first, 2)
    if groups > 1:
        forward_hidden(0, 1, groups - 2)
        forward_hidden(1, 1, groups - 2)
    for c in range(owners):
        arrive[("x", 0 if c < owners // 2 else 1, half, c)].wait_recv()
    keep(n - 1, 1)

    def pass_on(s, g):
        for d in ways(s, g):
            arrive[("h", d, s, g)].wait_recv()
        if s < half:
            for d in ways(s + 1, g):
                forward_hidden(d, s + 1, g)

    for g in range(groups - 2):
        pass_on(1, g)
    hidden(n - 1, 1)
    forward_hidden(0, 1, groups - 1)
    forward_hidden(1, 1, groups - 1)
    down(0, 0)
    arrive[("n", 0, half)].wait_recv()
    total = counts[owners]
    for j in range(1, n):
        total = total + counts[owners + j]
    factor_ref[...] = 2.0 / total
    for s in range(1, half + 1):
        for g in range(groups):
            if s > 1 or g >= groups - 2:
                pass_on(s, g)
        down(0, s)
        if s < half:
            down(1, s)
    for copy in pending:
        copy.wait_send()
    for copy in stores:
        copy.wait()


def gather(routes_t, slots_t, tokens, gate_rows, up_rows, n, owners):
    width = tokens.shape[1]
    units = gate_rows.shape[0]
    block = owners * CAP
    half = n // 2
    vmem = pl.BlockSpec(memory_space=pltpu.VMEM)
    hbm = pl.BlockSpec(memory_space=pl.ANY)
    rows = n * block
    dma = pltpu.SemaphoreType.DMA
    return pl.pallas_call(
        functools.partial(gather_kernel, n, owners),
        out_shape=(
            jax.ShapeDtypeStruct((rows, width), jnp.bfloat16),
            jax.ShapeDtypeStruct((n, units, units), jnp.float32),
            jax.ShapeDtypeStruct((8, 128), jnp.float32),
        ),
        in_specs=[vmem, vmem, vmem, hbm, hbm],
        out_specs=(hbm, vmem, vmem),
        scratch_shapes=[
            pltpu.VMEM((rows, width), jnp.bfloat16),
            pltpu.VMEM((block - CAP, width), jnp.bfloat16),
            pltpu.VMEM((units, width), jnp.bfloat16),
            pltpu.VMEM((units, width), jnp.bfloat16),
            pltpu.VMEM((2 * block, units), jnp.float32),
            pltpu.VMEM((2 * block, units), jnp.float32),
            pltpu.VMEM((n, rows, units), jnp.bfloat16),
            pltpu.VMEM((rows, units), jnp.bfloat16),
            pltpu.VMEM((owners + n, 8, 128), jnp.float32),
            pltpu.VMEM((owners, 8, 128), jnp.float32),
            dma((2,)),
            dma((n,)),
            dma((owners,)),
            dma((owners,)),
            dma((owners,)),
            dma((owners,)),
            dma((2, half + 1, owners)),
            dma((2, half + 1, owners)),
            dma((2, half + 1, 4)),
            dma((2, half + 1, 4)),
            dma((2, half + 1)),
            dma((2, half + 1)),
        ],
        compiler_params=pltpu.CompilerParams(
            collective_id=0, has_side_effects=True, vmem_limit_bytes=60 * 1024 * 1024
        ),
        cost_estimate=pl.CostEstimate(
            flops=4 * rows * width * units, bytes_accessed=6 * rows * width, transcendentals=rows * units
        ),
    )(routes_t, slots_t, tokens, gate_rows, up_rows)


def gram_kernel(place_ref, cols_ref, rows_ref, factor_ref, out_ref, turned):
    @pl.when(pl.program_id(0) == 0)
    def _():
        turned[...] = cols_ref[...].T

    out_ref[...] = factor_ref[0:1, 0:1] * jnp.dot(
        turned[...], rows_ref[...], preferred_element_type=jnp.float32
    )


def gram(rows, factor, place, col_count):
    depth, width = rows.shape
    tile = 512 if width % 512 == 0 else 128
    if col_count % 128 == 0:
        columns = rows
        spec = pl.BlockSpec((depth, col_count), lambda j, p: (0, p[0]))
    else:
        columns = lax.dynamic_slice_in_dim(rows, place * col_count, col_count, 1)
        spec = pl.BlockSpec((depth, col_count), lambda j, p: (0, 0))
    return pl.pallas_call(
        gram_kernel,
        out_shape=jax.ShapeDtypeStruct((col_count, width), jnp.float32),
        grid_spec=pltpu.PrefetchScalarGridSpec(
            num_scalar_prefetch=1,
            grid=(width // tile,),
            in_specs=[
                spec,
                pl.BlockSpec((depth, tile), lambda j, p: (0, j)),
                pl.BlockSpec((8, 128), lambda j, p: (0, 0)),
            ],
            out_specs=pl.BlockSpec((col_count, tile), lambda j, p: (0, j)),
            scratch_shapes=[pltpu.VMEM((col_count, depth), jnp.bfloat16)],
        ),
        compiler_params=pltpu.CompilerParams(vmem_limit_bytes=48 * 1024 * 1024),
        cost_estimate=pl.CostEstimate(
            flops=2 * depth * col_count * width, bytes_accessed=4 * col_count * width, transcendentals=0
        ),
    )(place.reshape(1), columns, rows, factor)


def local(tokens, routes, slot_ids, gate_weight, up_weight):
    width = tokens.shape[1]
    owners = lax.axis_size("expert")
    data_count = lax.axis_size("dp")
    rows, down, factor = gather(
        routes.T, slot_ids.T, tokens, gate_weight[0], up_weight[0], data_count, owners
    )
    place = lax.axis_index("dp").astype(jnp.int32)
    input_block = gram(rows, factor, place, width // data_count)
    down = jnp.transpose(down, (1, 0, 2)).reshape(down.shape[1], -1) * factor[0, 0]
    return (input_block[None], down[None])


def solution(mesh):
    in_specs = (
        P(("dp", "expert"), None),
        P(("dp", "expert"), None),
        P(("dp", "expert"), None),
        P("expert", "dp", None),
        P("expert", "dp", None),
    )
    out_specs = (P("expert", "dp", None), P("expert", "dp", None))
    return jax.shard_map(local, mesh=mesh, in_specs=in_specs, out_specs=out_specs, check_vma=False)
```

time: 159 us -> 130 us (0.82)
  blocking collectives: 41.3 us -> 0 us
  Pallas kernels: 81.2 us -> 121 us
  matrix products: 17.5 us -> 0 us
  between operations: 14.8 us -> 0.65 us
  local copies, waits for them, and re-layouts: 2.41 us -> 5.88 us
    psum x1 -> x0, blocking collectives: 41.3 us -> none  [local(): totals = lax.psum(local_counts, ('dp', 'expert'))]
    pallas_call x1, Pallas kernels: 81.2 us -> 103 us  [gather(): pl.pallas_call(functools.partial(gather_kernel, n, owners), out_shape=(ja...]
    pallas_call x0 -> x1, Pallas kernels: none -> 17.8 us  [gram(): pl.pallas_call(gram_kernel, out_shape=jax.ShapeDtypeStruct((col_count, wi...]
    dot_general x2 -> x0, matrix products: 17.5 us -> none  [the longest x1 15 us: local(): lax.dot_general(columns, rows, (((0,), (0,)), ((), ())), preferred_elemen...]
    mul x0 -> x1, other arithmetic: none -> 2.42 us  [local(): jnp.transpose(down, (1, 0, 2)).reshape(down.shape[1], -1) * factor[0, 0]]
    mul x0 -> x1, local copies, waits for them, and re-layouts: none -> 1.81 us  [local(): jnp.transpose(down, (1, 0, 2)).reshape(down.shape[1], -1) * factor[0, 0]]
  transfers between devices with their start and end apart: 1 -> 0, of which waited for: 0 -> 0; matrix products, arithmetic and copies ran while one was open for 10% -> 0% of each run, Pallas kernels for 0% -> 0%
where the time goes in v2:
time: 130 us
  Pallas kernels  121 us (93%)
  local copies, waits for them, and re-layouts  5.88 us (5%)
  other arithmetic  2.42 us (2%)
    pallas_call x1, Pallas kernels, gather(): pl.pallas_call(functools.partial(gather_kernel, n, owners), out_shape=(ja...  103 us
    pallas_call x1, Pallas kernels, gram(): pl.pallas_call(gram_kernel, out_shape=jax.ShapeDtypeStruct((col_count, wi...  17.8 us
    unnamed x3, local copies, waits for them, and re-layouts  2.88 us

profile of v2, /device:TPU:0, one launch (start us, length us, event | category | flops | bytes accessed | tf_op | source)
XLA Modules:
  0.0 129.7 jit_solution(12135788270524827849)
XLA Ops:
  0.6 103.0 %shard_map.68 = (bf16[512,7168]{1,0:T(8,128)(2,1)}, f32[8,256,256]{2,1,0:T(8,128)}, f32[8,128]{1,0:T(8,128)}) custom-call(s32[8,256]{1,0:T(8,128)} %bitcast.14, s32[8,256]{1,0:T(8,128)} %bitcast.15, bf16[256,7168]{1,0:T(8,128)(2,1)} %tok_ref.1, bf16[256,7168]{1,0:T(8,128)(2,1)} %bitcast.12, bf16[256,7168]{1,0:T(8,128)(2,1)} %bitcast.13), custom_call_target="tpu_custom_call" | custom-call | flops 3758096384 | bytes 22020096 | tf_op jit(solution)/shard_map/pallas_call | solution.py:249
  103.6 1.2 slice.3
  104.8 2.4 %multiply_bitcast_fusion = f32[256,8,256]{2,0,1:T(8,128)S(1)} fusion(f32[8,256,256]{2,1,0:T(8,128)} %get-tuple-element.7, f32[]{:T(128)} %bitcast.6), kind=kLoop, calls=%fused_computation | loop fusion | flops 524288 | bytes 4194308 | tf_op jit(solution)/shard_map/mul | solution.py:340
  107.2 1.8 %copy.7 = f32[256,8,256]{0,2,1:T(8,128)} copy(f32[256,8,256]{2,0,1:T(8,128)S(1)} %multiply_bitcast_fusion) | data formatting | bytes 4194304 | tf_op jit(solution)/shard_map/mul | solution.py:340
  109.1 0.0 copy-start
  109.1 2.9 %copy.8 = f32[1,256,2048]{2,1,0:T(8,128)} copy(f32[1,256,2048]{1,2,0:T(8,128)} %bitcast.11) | data formatting | bytes 4194304
  111.9 0.0 copy-done
  111.9 17.8 %shard_map.69 = f32[896,7168]{1,0:T(8,128)} custom-call(s32[1]{0:T(128)} %bitcast.place_ref, bf16[512,7168]{1,0:T(8,128)(2,1)} %get-tuple-element.5.cols_ref.rows_ref, bf16[512,7168]{1,0:T(8,128)(2,1)} %get-tuple-element.5.cols_ref.rows_ref, f32[8,128]{1,0:T(8,128)S(1)} %copy-done), custom_call_target="tpu_custom_call" | custom-call | flops 6576668672 | bytes 25690112 | tf_op jit(solution)/shard_map/pallas_call | solution.py:310
Async XLA Ops:
  109.1 2.9 %copy-start = (f32[8,128]{1,0:T(8,128)S(1)}, f32[8,128]{1,0:T(8,128)}, u32[]{:S(2)}) copy-start(f32[8,128]{1,0:T(8,128)} %get-tuple-element.6.factor_ref) | copy-start | bytes 12292

commit v3 on v2

--- a/solution.py
+++ b/solution.py
@@ -15,7 +15,8 @@
     return ((e // 2 + k // 2) % (owners // 2)) * 2 + (e + k) % 2
 
 
-def gather_kernel(n, owners, route_ref, slot_ref, tok_ref, gate_ref, up_ref, x_ref, down_ref, factor_ref,
+def gather_kernel(n, owners, route_ref, slot_ref, tok_ref, gate_ref, up_ref,
+                  x_ref, down_ref, factor_ref, turned_ref,
                   xbuf, sbuf, wg, wu, acc_g, acc_u, hbuf, mine, counts, held_counts,
                   w_sem, out_sem, ex_send, ex_recv, cx_send, cx_recv,
                   ring_send, ring_recv, hid_send, hid_recv, cnt_send, cnt_recv):
@@ -149,9 +150,15 @@
         for r in range(n):
             own = slot_of[(offsets[j] + offsets[r]) % n]
             mine[r * block:(r + 1) * block, :] = hbuf[0, own * block:(own + 1) * block, :]
-        down_ref[at((pos + offsets[j]) % n)] = lax.dot_general(
+        part = factor_ref[0:1, 0:1] * lax.dot_general(
             mine[...], hbuf[j], (((0,), (0,)), ((), ())), preferred_element_type=jnp.float32
         )
+        place = at((pos + offsets[j]) % n)
+        if len(down_ref.shape) == 2:
+            units = down_ref.shape[0]
+            down_ref[:, pl.ds(pl.multiple_of(place * units, units), units)] = part
+        else:
+            down_ref[place] = part
 
     stores = []
 
@@ -218,16 +225,22 @@
     hidden(n - 1, 1)
     forward_hidden(0, 1, groups - 1)
     forward_hidden(1, 1, groups - 1)
-    down(0, 0)
     arrive[("n", 0, half)].wait_recv()
     total = counts[owners]
     for j in range(1, n):
         total = total + counts[owners + j]
     factor_ref[...] = 2.0 / total
+    down(0, 0)
     for s in range(1, half + 1):
         for g in range(groups):
             if s > 1 or g >= groups - 2:
                 pass_on(s, g)
+        if s == 2:
+            count = turned_ref.shape[0]
+            if count == width // n:
+                turned_ref[...] = xbuf[:, pl.ds(pl.multiple_of(me * count, 128), count)].T
+            else:
+                turned_ref[...] = jnp.zeros(turned_ref.shape, jnp.bfloat16)
         down(0, s)
         if s < half:
             down(1, s)
@@ -250,11 +263,12 @@
         functools.partial(gather_kernel, n, owners),
         out_shape=(
             jax.ShapeDtypeStruct((rows, width), jnp.bfloat16),
-            jax.ShapeDtypeStruct((n, units, units), jnp.float32),
+            jax.ShapeDtypeStruct((units, n * units) if units % 128 == 0 else (n, units, units), jnp.float32),
             jax.ShapeDtypeStruct((8, 128), jnp.float32),
+            jax.ShapeDtypeStruct((width // n, rows) if (width // n) % 128 == 0 else (8, 128), jnp.bfloat16),
         ),
         in_specs=[vmem, vmem, vmem, hbm, hbm],
-        out_specs=(hbm, vmem, vmem),
+        out_specs=(hbm, vmem, vmem, vmem),
         scratch_shapes=[
             pltpu.VMEM((rows, width), jnp.bfloat16),
             pltpu.VMEM((block - CAP, width), jnp.bfloat16),
@@ -288,57 +302,97 @@
     )(routes_t, slots_t, tokens, gate_rows, up_rows)
 
 
-def gram_kernel(place_ref, cols_ref, rows_ref, factor_ref, out_ref, turned):
-    @pl.when(pl.program_id(0) == 0)
-    def _():
-        turned[...] = cols_ref[...].T
-
-    out_ref[...] = factor_ref[0:1, 0:1] * jnp.dot(
-        turned[...], rows_ref[...], preferred_element_type=jnp.float32
-    )
-
-
-def gram(rows, factor, place, col_count):
+def gram_kernel(tile, pieces, turned_ref, rows_ref, factor_ref, down_in, out_ref, down_out,
+                held, parts, in_sem, out_sem, down_sem):
+    width = rows_ref.shape[1]
+    slots, count = parts.shape[0], parts.shape[1]
+    steps = width // tile
+    piece = count // pieces
+
+    def load(j):
+        cols = pl.ds(pl.multiple_of(j * tile, tile), tile)
+        return pltpu.make_async_copy(rows_ref.at[:, cols], held.at[:, cols], in_sem.at[j])
+
+    def store(j, i):
+        b = j % slots
+        rows = pl.ds(i * piece, piece)
+        cols = pl.ds(pl.multiple_of(j * tile, tile), tile)
+        return pltpu.make_async_copy(parts.at[b, rows], out_ref.at[rows, cols], out_sem.at[b, i])
+
+    for j in range(steps):
+        load(j).start()
+    down_copy = pltpu.make_async_copy(down_in, down_out, down_sem.at[0])
+    down_copy.start()
+
+    def body(j, carry):
+        load(j).wait()
+
+        @pl.when(j >= slots)
+        def _():
+            for i in range(pieces):
+                store(j - slots, i).wait()
+
+        cols = pl.ds(pl.multiple_of(j * tile, tile), tile)
+        for i in range(pieces):
+            rows = slice(i * piece, (i + 1) * piece)
+            parts[j % slots, rows] = factor_ref[0:1, 0:1] * jnp.dot(
+                turned_ref[rows, :], held[:, cols], preferred_element_type=jnp.float32
+            )
+            store(j, i).start()
+        return carry
+
+    lax.fori_loop(0, steps, body, 0)
+    for j in range(max(0, steps - slots), steps):
+        for i in range(pieces):
+            store(j, i).wait()
+    down_copy.wait()
+
+
+def gram(turned, rows, factor, down):
     depth, width = rows.shape
+    count = turned.shape[0]
     tile = 512 if width % 512 == 0 else 128
-    if col_count % 128 == 0:
-        columns = rows
-        spec = pl.BlockSpec((depth, col_count), lambda j, p: (0, p[0]))
-    else:
-        columns = lax.dynamic_slice_in_dim(rows, place * col_count, col_count, 1)
-        spec = pl.BlockSpec((depth, col_count), lambda j, p: (0, 0))
+    pieces = 2 if count % 16 == 0 else 1
+    slots = 4
+    vmem = pl.BlockSpec(memory_space=pltpu.VMEM)
+    hbm = pl.BlockSpec(memory_space=pl.ANY)
+    dma = pltpu.SemaphoreType.DMA
     return pl.pallas_call(
-        gram_kernel,
-        out_shape=jax.ShapeDtypeStruct((col_count, width), jnp.float32),
-        grid_spec=pltpu.PrefetchScalarGridSpec(
-            num_scalar_prefetch=1,
-            grid=(width // tile,),
-            in_specs=[
-                spec,
-                pl.BlockSpec((depth, tile), lambda j, p: (0, j)),
-                pl.BlockSpec((8, 128), lambda j, p: (0, 0)),
-            ],
-            out_specs=pl.BlockSpec((col_count, tile), lambda j, p: (0, j)),
-            scratch_shapes=[pltpu.VMEM((col_count, depth), jnp.bfloat16)],
+        functools.partial(gram_kernel, tile, pieces),
+        out_shape=(
+            jax.ShapeDtypeStruct((count, width), jnp.float32),
+            jax.ShapeDtypeStruct(down.shape, jnp.float32),
         ),
-        compiler_params=pltpu.CompilerParams(vmem_limit_bytes=48 * 1024 * 1024),
+        in_specs=[vmem, hbm, vmem, hbm],
+        out_specs=(hbm, hbm),
+        scratch_shapes=[
+            pltpu.VMEM((depth, width), jnp.bfloat16),
+            pltpu.VMEM((slots, count, tile), jnp.float32),
+            dma((width // tile,)),
+            dma((slots, pieces)),
+            dma((1,)),
+        ],
+        compiler_params=pltpu.CompilerParams(vmem_limit_bytes=60 * 1024 * 1024),
         cost_estimate=pl.CostEstimate(
-            flops=2 * depth * col_count * width, bytes_accessed=4 * col_count * width, transcendentals=0
+            flops=2 * depth * count * width, bytes_accessed=4 * count * width, transcendentals=0
         ),
-    )(place.reshape(1), columns, rows, factor)
+    )(turned, rows, factor, down)
 
 
 def local(tokens, routes, slot_ids, gate_weight, up_weight):
     width = tokens.shape[1]
     owners = lax.axis_size("expert")
     data_count = lax.axis_size("dp")
-    rows, down, factor = gather(
+    rows, down, factor, turned = gather(
         routes.T, slot_ids.T, tokens, gate_weight[0], up_weight[0], data_count, owners
     )
-    place = lax.axis_index("dp").astype(jnp.int32)
-    input_block = gram(rows, factor, place, width // data_count)
-    down = jnp.transpose(down, (1, 0, 2)).reshape(down.shape[1], -1) * factor[0, 0]
-    return (input_block[None], down[None])
+    count = width // data_count
+    if turned.shape[0] != count:
+        turned = lax.dynamic_slice_in_dim(rows, lax.axis_index("dp") * count, count, 1).T
+    if down.ndim == 3:
+        down = jnp.transpose(down, (1, 0, 2)).reshape(down.shape[1], -1)
+    input_block, down_block = gram(turned, rows, factor, down)
+    return (input_block[None], down_block[None])
 
 
 def solution(mesh):

time: 130 us -> 170 us (1.31)
  Pallas kernels: 121 us -> 169 us
  local copies, waits for them, and re-layouts: 5.88 us -> 0 us
  other arithmetic: 2.42 us -> 0 us
    pallas_call x1, Pallas kernels: 17.8 us -> 66 us  [gram(): pl.pallas_call(functools.partial(gram_kernel, tile, pieces), out_shape=(j...]
    unnamed x3 -> x0, local copies, waits for them, and re-layouts: 2.88 us -> none
    mul x1 -> x0, other arithmetic: 2.42 us -> none  [local(): jnp.transpose(down, (1, 0, 2)).reshape(down.shape[1], -1) * factor[0, 0]]
    mul x1 -> x0, local copies, waits for them, and re-layouts: 1.81 us -> none  [local(): jnp.transpose(down, (1, 0, 2)).reshape(down.shape[1], -1) * factor[0, 0]]
where the time goes in v3:
time: 170 us
  Pallas kernels  169 us (99%)
    pallas_call x1, Pallas kernels, gather(): pl.pallas_call(functools.partial(gather_kernel, n, owners), out_shape=(ja...  103 us
    pallas_call x1, Pallas kernels, gram(): pl.pallas_call(functools.partial(gram_kernel, tile, pieces), out_shape=(j...  66 us

profile of v3, /device:TPU:0, one launch (start us, length us, event | category | flops | bytes accessed | tf_op | source)
XLA Modules:
  0.0 169.9 jit_solution(4418700389394222884)
XLA Ops:
  0.6 103.3 %shard_map.68 = (bf16[512,7168]{1,0:T(8,128)(2,1)}, f32[256,2048]{1,0:T(8,128)}, f32[8,128]{1,0:T(8,128)}, bf16[896,512]{1,0:T(8,128)(2,1)}) custom-call(s32[8,256]{1,0:T(8,128)} %bitcast.8, s32[8,256]{1,0:T(8,128)} %bitcast.9, bf16[256,7168]{1,0:T(8,128)(2,1)} %tok_ref.1, bf16[256,7168]{1,0:T(8,128)(2,1)} %bitcast.6, bf16[256,7168]{1,0:T(8,128)(2,1)} %bitcast.7), custom_call_target="tpu_custom_call" | custom-call | flops 3758096384 | bytes 22020096 | tf_op jit(solution)/shard_map/pallas_call | solution.py:262
  103.9 66.0 %shard_map.69 = (f32[896,7168]{1,0:T(8,128)}, f32[256,2048]{1,0:T(8,128)}) custom-call(bf16[896,512]{1,0:T(8,128)(2,1)} %get-tuple-element.8.turned_ref, bf16[512,7168]{1,0:T(8,128)(2,1)} %get-tuple-element.9.rows_ref, f32[8,128]{1,0:T(8,128)} %get-tuple-element.10.factor_ref, f32[256,2048]{1,0:T(8,128)} %get-tuple-element.11.down_in), custom_call_target="tpu_custom_call" | custom-call | flops 6576668672 | bytes 25690112 | tf_op jit(solution)/shard_map/pallas_call | solution.py:360

commit v4 on v3

--- a/solution.py
+++ b/solution.py
@@ -17,8 +17,8 @@
 
 def gather_kernel(n, owners, route_ref, slot_ref, tok_ref, gate_ref, up_ref,
                   x_ref, down_ref, factor_ref, turned_ref,
-                  xbuf, sbuf, wg, wu, acc_g, acc_u, hbuf, mine, counts, held_counts,
-                  w_sem, out_sem, ex_send, ex_recv, cx_send, cx_recv,
+                  xbuf, sbuf, tok, wg, wu, acc_g, acc_u, hbuf, mine, counts, held_counts,
+                  tok_sem, w_sem, out_sem, ex_send, ex_recv, cx_send, cx_recv,
                   ring_send, ring_recv, hid_send, hid_recv, cnt_send, cnt_recv):
     width = tok_ref.shape[1]
     block = owners * CAP
@@ -34,6 +34,15 @@
 
     near = (at((pos + 1) % n), at((pos + n - 1) % n))
 
+    step_cols = 1024 if width % 1024 == 0 else 128
+
+    def panel(j):
+        cols = pl.ds(pl.multiple_of(j * step_cols, step_cols), step_cols)
+        return pltpu.make_async_copy(tok_ref.at[:, cols], tok.at[:, cols], tok_sem.at[j])
+
+    for j in range(width // step_cols):
+        panel(j).start()
+
     barrier = pltpu.get_barrier_semaphore()
     for k in range(1, owners):
         pl.semaphore_signal(barrier, inc=1, device_id=(me, peer(e, k, owners)), device_id_type=MESH)
@@ -44,8 +53,6 @@
         pltpu.make_async_copy(gate_ref, wg, w_sem.at[0]),
         pltpu.make_async_copy(up_ref, wu, w_sem.at[1]),
     ]
-    for load in loads:
-        load.start()
 
     slot_rows = lax.broadcasted_iota(jnp.int32, (CAP, tok_ref.shape[0]), 0)
     picks = []
@@ -59,11 +66,10 @@
         counts[k] = jnp.broadcast_to(jnp.sum(pick, axis=(0, 1), keepdims=True), counts.shape[1:])
     hot = jnp.concatenate(picks, axis=0).astype(jnp.bfloat16)
 
-    step_cols = 1024 if width % 1024 == 0 else 128
-
     def dispatch(j, carry):
         cols = pl.ds(pl.multiple_of(j * step_cols, step_cols), step_cols)
-        rows = jnp.dot(hot, tok_ref[:, cols], preferred_element_type=jnp.float32)
+        panel(j).wait()
+        rows = jnp.dot(hot, tok[:, cols], preferred_element_type=jnp.float32)
         rows = rows.astype(jnp.bfloat16)
         xbuf[0:CAP, cols] = rows[0:CAP]
         sbuf[:, cols] = rows[CAP:]
@@ -71,6 +77,8 @@
 
     lax.fori_loop(0, width // step_cols, dispatch, 0)
     pl.semaphore_wait(barrier, owners + 1)
+    for load in loads:
+        load.start()
 
     pending = []
     arrive = {}
@@ -267,11 +275,12 @@
             jax.ShapeDtypeStruct((8, 128), jnp.float32),
             jax.ShapeDtypeStruct((width // n, rows) if (width // n) % 128 == 0 else (8, 128), jnp.bfloat16),
         ),
-        in_specs=[vmem, vmem, vmem, hbm, hbm],
+        in_specs=[vmem, vmem, hbm, hbm, hbm],
         out_specs=(hbm, vmem, vmem, vmem),
         scratch_shapes=[
             pltpu.VMEM((rows, width), jnp.bfloat16),
             pltpu.VMEM((block - CAP, width), jnp.bfloat16),
+            pltpu.VMEM(tokens.shape, jnp.bfloat16),
             pltpu.VMEM((units, width), jnp.bfloat16),
             pltpu.VMEM((units, width), jnp.bfloat16),
             pltpu.VMEM((2 * block, units), jnp.float32),
@@ -280,6 +289,7 @@
             pltpu.VMEM((rows, units), jnp.bfloat16),
             pltpu.VMEM((owners + n, 8, 128), jnp.float32),
             pltpu.VMEM((owners, 8, 128), jnp.float32),
+            dma((width // (1024 if width % 1024 == 0 else 128),)),
             dma((2,)),
             dma((n,)),
             dma((owners,)),
@@ -303,7 +313,7 @@
 
 
 def gram_kernel(tile, pieces, turned_ref, rows_ref, factor_ref, down_in, out_ref, down_out,
-                held, parts, in_sem, out_sem, down_sem):
+                held, parts, turned, down_held, in_sem, out_sem, own_sem):
     width = rows_ref.shape[1]
     slots, count = parts.shape[0], parts.shape[1]
     steps = width // tile
@@ -319,10 +329,14 @@
         cols = pl.ds(pl.multiple_of(j * tile, tile), tile)
         return pltpu.make_async_copy(parts.at[b, rows], out_ref.at[rows, cols], out_sem.at[b, i])
 
+    turned_load = pltpu.make_async_copy(turned_ref, turned, own_sem.at[0])
+    down_load = pltpu.make_async_copy(down_in, down_held, own_sem.at[1])
+    down_store = pltpu.make_async_copy(down_held, down_out, own_sem.at[2])
+    turned_load.start()
     for j in range(steps):
         load(j).start()
-    down_copy = pltpu.make_async_copy(down_in, down_out, down_sem.at[0])
-    down_copy.start()
+    down_load.start()
+    turned_load.wait()
 
     def body(j, carry):
         load(j).wait()
@@ -336,16 +350,20 @@
         for i in range(pieces):
             rows = slice(i * piece, (i + 1) * piece)
             parts[j % slots, rows] = factor_ref[0:1, 0:1] * jnp.dot(
-                turned_ref[rows, :], held[:, cols], preferred_element_type=jnp.float32
+                turned[rows, :], held[:, cols], preferred_element_type=jnp.float32
             )
             store(j, i).start()
         return carry
 
-    lax.fori_loop(0, steps, body, 0)
+    early = min(slots, steps)
+    lax.fori_loop(0, early, body, 0)
+    down_load.wait()
+    down_store.start()
+    lax.fori_loop(early, steps, body, 0)
     for j in range(max(0, steps - slots), steps):
         for i in range(pieces):
             store(j, i).wait()
-    down_copy.wait()
+    down_store.wait()
 
 
 def gram(turned, rows, factor, down):
@@ -363,14 +381,16 @@
             jax.ShapeDtypeStruct((count, width), jnp.float32),
             jax.ShapeDtypeStruct(down.shape, jnp.float32),
         ),
-        in_specs=[vmem, hbm, vmem, hbm],
+        in_specs=[hbm, hbm, vmem, hbm],
         out_specs=(hbm, hbm),
         scratch_shapes=[
             pltpu.VMEM((depth, width), jnp.bfloat16),
             pltpu.VMEM((slots, count, tile), jnp.float32),
+            pltpu.VMEM(turned.shape, jnp.bfloat16),
+            pltpu.VMEM(down.shape, jnp.float32),
             dma((width // tile,)),
             dma((slots, pieces)),
-            dma((1,)),
+            dma((3,)),
         ],
         compiler_params=pltpu.CompilerParams(vmem_limit_bytes=60 * 1024 * 1024),
         cost_estimate=pl.CostEstimate(

time: 170 us -> 118 us (0.69)
  Pallas kernels: 169 us -> 117 us
    pallas_call x1, Pallas kernels: 66 us -> 14.2 us  [gram(): pl.pallas_call(functools.partial(gram_kernel, tile, pieces), out_shape=(j...]
where the time goes in v4:
time: 118 us
  Pallas kernels  117 us (99%)
    pallas_call x1, Pallas kernels, gather(): pl.pallas_call(functools.partial(gather_kernel, n, owners), out_shape=(ja...  103 us
    pallas_call x1, Pallas kernels, gram(): pl.pallas_call(functools.partial(gram_kernel, tile, pieces), out_shape=(j...  14.2 us

profile of v4, /device:TPU:0, one launch (start us, length us, event | category | flops | bytes accessed | tf_op | source)
XLA Modules:
  0.0 117.6 jit_solution(10852400097040687021)
XLA Ops:
  0.6 102.8 %shard_map.68 = (bf16[512,7168]{1,0:T(8,128)(2,1)}, f32[256,2048]{1,0:T(8,128)}, f32[8,128]{1,0:T(8,128)}, bf16[896,512]{1,0:T(8,128)(2,1)}) custom-call(s32[8,256]{1,0:T(8,128)} %bitcast.8, s32[8,256]{1,0:T(8,128)} %bitcast.9, bf16[256,7168]{1,0:T(8,128)(2,1)} %tok_ref.1, bf16[256,7168]{1,0:T(8,128)(2,1)} %bitcast.6, bf16[256,7168]{1,0:T(8,128)(2,1)} %bitcast.7), custom_call_target="tpu_custom_call" | custom-call | flops 3758096384 | bytes 22020096 | tf_op jit(solution)/shard_map/pallas_call | solution.py:270
  103.4 14.2 %shard_map.69 = (f32[896,7168]{1,0:T(8,128)}, f32[256,2048]{1,0:T(8,128)}) custom-call(bf16[896,512]{1,0:T(8,128)(2,1)} %get-tuple-element.8.turned_ref, bf16[512,7168]{1,0:T(8,128)(2,1)} %get-tuple-element.9.rows_ref, f32[8,128]{1,0:T(8,128)} %get-tuple-element.10.factor_ref, f32[256,2048]{1,0:T(8,128)} %get-tuple-element.11.down_in), custom_call_target="tpu_custom_call" | custom-call | flops 6576668672 | bytes 25690112 | tf_op jit(solution)/shard_map/pallas_call | solution.py:378

commit v5 on v4

--- a/solution.py
+++ b/solution.py
@@ -17,8 +17,8 @@
 
 def gather_kernel(n, owners, route_ref, slot_ref, tok_ref, gate_ref, up_ref,
                   x_ref, down_ref, factor_ref, turned_ref,
-                  xbuf, sbuf, tok, wg, wu, acc_g, acc_u, hbuf, mine, counts, held_counts,
-                  tok_sem, w_sem, out_sem, ex_send, ex_recv, cx_send, cx_recv,
+                  xbuf, sbuf, tok, wg, wu, acc_g, acc_u, hbuf, mine, turned, dpart, counts, held_counts,
+                  tok_sem, w_sem, out_sem, down_sem, ex_send, ex_recv, cx_send, cx_recv,
                   ring_send, ring_recv, hid_send, hid_recv, cnt_send, cnt_recv):
     width = tok_ref.shape[1]
     block = owners * CAP
@@ -75,11 +75,6 @@
         sbuf[:, cols] = rows[CAP:]
         return carry
 
-    lax.fori_loop(0, width // step_cols, dispatch, 0)
-    pl.semaphore_wait(barrier, owners + 1)
-    for load in loads:
-        load.start()
-
     pending = []
     arrive = {}
 
@@ -91,6 +86,23 @@
         copy.start()
         pending.append(copy)
         arrive[key] = copy
+
+    panels = width // step_cols
+    cut = (panels + 1) // 2
+    lax.fori_loop(0, cut, dispatch, 0)
+    pl.semaphore_wait(barrier, owners + 1)
+    left, right = pl.ds(0, cut * step_cols), pl.ds(cut * step_cols, (panels - cut) * step_cols)
+    for d in (0, 1):
+        send(("x", d, 1, "first"), xbuf.at[pl.ds(0, CAP), left], xbuf.at[pl.ds((1 + d) * block, CAP), left],
+             ring_send.at[d, 0, 0], ring_recv.at[d, 0, 0], (near[d], e))
+    lax.fori_loop(cut, panels, dispatch, 0)
+    for d in (0, 1):
+        send(("x", d, 1, 0), xbuf.at[pl.ds(0, CAP), right], xbuf.at[pl.ds((1 + d) * block, CAP), right],
+             ring_send.at[d, 1, 0], ring_recv.at[d, 1, 0], (near[d], e))
+    for load in loads:
+        load.start()
+
+    stores = []
 
     for k in range(1, owners):
         other = (me, peer(e, k, owners))
@@ -162,13 +174,15 @@
             mine[...], hbuf[j], (((0,), (0,)), ((), ())), preferred_element_type=jnp.float32
         )
         place = at((pos + offsets[j]) % n)
+        dpart[j] = part
         if len(down_ref.shape) == 2:
             units = down_ref.shape[0]
-            down_ref[:, pl.ds(pl.multiple_of(place * units, units), units)] = part
+            target = down_ref.at[:, pl.ds(pl.multiple_of(place * units, units), units)]
         else:
-            down_ref[place] = part
-
-    stores = []
+            target = down_ref.at[place]
+        copy = pltpu.make_async_copy(dpart.at[j], target, down_sem.at[j])
+        copy.start()
+        stores.append(copy)
 
     def keep(first, count):
         rows = pl.ds(first * block, count * block)
@@ -182,9 +196,14 @@
                 if c > 0:
                     arrive[("x", 0, 0, c)].wait_recv()
             else:
+                if s == 2 and c == 0:
+                    arrive[("x", 0, 1, "first")].wait_recv()
+                    arrive[("x", 1, 1, "first")].wait_recv()
                 arrive[("x", 0, s - 1, c)].wait_recv()
                 arrive[("x", 1, s - 1, c)].wait_recv()
-            if s < half:
+            if s == 1 and c == 0:
+                pass
+            elif s < half:
                 forward(0, s, c)
                 forward(1, s, c)
             else:
@@ -246,9 +265,10 @@
         if s == 2:
             count = turned_ref.shape[0]
             if count == width // n:
-                turned_ref[...] = xbuf[:, pl.ds(pl.multiple_of(me * count, 128), count)].T
-            else:
-                turned_ref[...] = jnp.zeros(turned_ref.shape, jnp.bfloat16)
+                turned[...] = xbuf[:, pl.ds(pl.multiple_of(me * count, 128), count)].T
+                copy = pltpu.make_async_copy(turned, turned_ref, down_sem.at[n])
+                copy.start()
+                stores.append(copy)
         down(0, s)
         if s < half:
             down(1, s)
@@ -276,7 +296,7 @@
             jax.ShapeDtypeStruct((width // n, rows) if (width // n) % 128 == 0 else (8, 128), jnp.bfloat16),
         ),
         in_specs=[vmem, vmem, hbm, hbm, hbm],
-        out_specs=(hbm, vmem, vmem, vmem),
+        out_specs=(hbm, hbm, vmem, hbm),
         scratch_shapes=[
             pltpu.VMEM((rows, width), jnp.bfloat16),
             pltpu.VMEM((block - CAP, width), jnp.bfloat16),
@@ -287,11 +307,14 @@
             pltpu.VMEM((2 * block, units), jnp.float32),
             pltpu.VMEM((n, rows, units), jnp.bfloat16),
             pltpu.VMEM((rows, units), jnp.bfloat16),
+            pltpu.VMEM((width // n, rows) if (width // n) % 128 == 0 else (8, 128), jnp.bfloat16),
+            pltpu.VMEM((n, units, units), jnp.float32),
             pltpu.VMEM((owners + n, 8, 128), jnp.float32),
             pltpu.VMEM((owners, 8, 128), jnp.float32),
             dma((width // (1024 if width % 1024 == 0 else 128),)),
             dma((2,)),
             dma((n,)),
+            dma((n + 1,)),
             dma((owners,)),
             dma((owners,)),
             dma((owners,)),
@@ -333,13 +356,17 @@
     down_load = pltpu.make_async_copy(down_in, down_held, own_sem.at[1])
     down_store = pltpu.make_async_copy(down_held, down_out, own_sem.at[2])
     turned_load.start()
-    for j in range(steps):
+    ahead = min(3, steps)
+    for j in range(ahead):
         load(j).start()
-    down_load.start()
     turned_load.wait()
 
     def body(j, carry):
         load(j).wait()
+
+        @pl.when(j + ahead < steps)
+        def _():
+            load(j + ahead).start()
 
         @pl.when(j >= slots)
         def _():
@@ -355,11 +382,13 @@
             store(j, i).start()
         return carry
 
-    early = min(slots, steps)
+    early, late = min(slots, steps), max(min(slots, steps), steps - 3)
     lax.fori_loop(0, early, body, 0)
+    down_load.start()
+    lax.fori_loop(early, late, body, 0)
     down_load.wait()
     down_store.start()
-    lax.fori_loop(early, steps, body, 0)
+    lax.fori_loop(late, steps, body, 0)
     for j in range(max(0, steps - slots), steps):
         for i in range(pieces):
             store(j, i).wait()

time: 118 us -> 117 us (level)
  no operation moved by 1% of the time
where the time goes in v5:
time: 117 us
  Pallas kernels  116 us (99%)
    pallas_call x1, Pallas kernels, gather(): pl.pallas_call(functools.partial(gather_kernel, n, owners), out_shape=(ja...  102 us
    pallas_call x1, Pallas kernels, gram(): pl.pallas_call(functools.partial(gram_kernel, tile, pieces), out_shape=(j...  14.4 us

profile of v5, /device:TPU:0, one launch (start us, length us, event | category | flops | bytes accessed | tf_op | source)
XLA Modules:
  0.0 116.8 jit_solution(11696197697259257692)
XLA Ops:
  0.6 101.7 %shard_map.68 = (bf16[512,7168]{1,0:T(8,128)(2,1)}, f32[256,2048]{1,0:T(8,128)}, f32[8,128]{1,0:T(8,128)}, bf16[896,512]{1,0:T(8,128)(2,1)}) custom-call(s32[8,256]{1,0:T(8,128)} %bitcast.8, s32[8,256]{1,0:T(8,128)} %bitcast.9, bf16[256,7168]{1,0:T(8,128)(2,1)} %tok_ref.1, bf16[256,7168]{1,0:T(8,128)(2,1)} %bitcast.6, bf16[256,7168]{1,0:T(8,128)(2,1)} %bitcast.7), custom_call_target="tpu_custom_call" | custom-call | flops 3758096384 | bytes 22020096 | tf_op jit(solution)/shard_map/pallas_call | solution.py:290
  102.4 14.4 %shard_map.69 = (f32[896,7168]{1,0:T(8,128)}, f32[256,2048]{1,0:T(8,128)}) custom-call(bf16[896,512]{1,0:T(8,128)(2,1)} %get-tuple-element.8.turned_ref, bf16[512,7168]{1,0:T(8,128)(2,1)} %get-tuple-element.9.rows_ref, f32[8,128]{1,0:T(8,128)} %get-tuple-element.10.factor_ref, f32[256,2048]{1,0:T(8,128)} %get-tuple-element.11.down_in), custom_call_target="tpu_custom_call" | custom-call | flops 6576668672 | bytes 25690112 | tf_op jit(solution)/shard_map/pallas_call | solution.py:407

commit v6 on v5

--- a/solution.py
+++ b/solution.py
@@ -104,10 +104,13 @@
 
     stores = []
 
-    for k in range(1, owners):
+    def exchange(k):
         other = (me, peer(e, k, owners))
         send(("x", 0, 0, k), sbuf.at[pl.ds((k - 1) * CAP, CAP)], xbuf.at[pl.ds(k * CAP, CAP)],
              ex_send.at[k], ex_recv.at[k], other)
+
+    for k in range(1, owners - 1):
+        exchange(k)
     for k in range(1, owners):
         other = (me, peer(e, k, owners))
         send(("c", 0, k), counts.at[k], held_counts.at[k], cx_send.at[k], cx_recv.at[k], other)
@@ -140,7 +143,7 @@
              hid_send.at[d, s, g], hid_recv.at[d, s, g], (near[d], e))
 
     def ways(s, g):
-        return (0, 1) if s < half else (g % 2,)
+        return (0, 1) if s < half else ((0,) if g in (0, 3) else (1,))
 
     def forward_counts(d, s):
         send(("n", d, s), counts.at[owners + slot(d, s - 1)], counts.at[owners + slot(d, s)],
@@ -165,11 +168,15 @@
         out = (gate / (1.0 + jnp.exp(-gate)) * acc_u[0:rows, :]).astype(jnp.bfloat16)
         hbuf[0, base:base + rows, :] = out
 
-    def down(d, s):
-        j = slot(d, s)
+    def arrange(j):
         for r in range(n):
             own = slot_of[(offsets[j] + offsets[r]) % n]
             mine[r * block:(r + 1) * block, :] = hbuf[0, own * block:(own + 1) * block, :]
+
+    def down(d, s):
+        j = slot(d, s)
+        if s < half:
+            arrange(j)
         part = factor_ref[0:1, 0:1] * lax.dot_general(
             mine[...], hbuf[j], (((0,), (0,)), ((), ())), preferred_element_type=jnp.float32
         )
@@ -193,6 +200,11 @@
     for s in range(1, half + 1):
         for c in range(owners):
             if s == 1:
+                if c == owners - 2:
+                    held_back = arrive[("x", 0, 0, c)]
+                    held_back.wait_send()
+                    pending[:] = [copy for copy in pending if copy is not held_back]
+                    exchange(owners - 1)
                 if c > 0:
                     arrive[("x", 0, 0, c)].wait_recv()
             else:
@@ -259,6 +271,8 @@
     factor_ref[...] = 2.0 / total
     down(0, 0)
     for s in range(1, half + 1):
+        if s == half:
+            arrange(n - 1)
         for g in range(groups):
             if s > 1 or g >= groups - 2:
                 pass_on(s, g)

time: 117 us -> 117 us (level)
  no operation moved by 1% of the time
where the time goes in v6:
time: 117 us
  Pallas kernels  116 us (99%)
    pallas_call x1, Pallas kernels, gather(): pl.pallas_call(functools.partial(gather_kernel, n, owners), out_shape=(ja...  102 us
    pallas_call x1, Pallas kernels, gram(): pl.pallas_call(functools.partial(gram_kernel, tile, pieces), out_shape=(j...  14.4 us

profile of v6, /device:TPU:0, one launch (start us, length us, event | category | flops | bytes accessed | tf_op | source)
XLA Modules:
  0.0 116.6 jit_solution(4974261719443027933)
XLA Ops:
  0.6 101.5 %shard_map.68 = (bf16[512,7168]{1,0:T(8,128)(2,1)}, f32[256,2048]{1,0:T(8,128)}, f32[8,128]{1,0:T(8,128)}, bf16[896,512]{1,0:T(8,128)(2,1)}) custom-call(s32[8,256]{1,0:T(8,128)} %bitcast.8, s32[8,256]{1,0:T(8,128)} %bitcast.9, bf16[256,7168]{1,0:T(8,128)(2,1)} %tok_ref.1, bf16[256,7168]{1,0:T(8,128)(2,1)} %bitcast.6, bf16[256,7168]{1,0:T(8,128)(2,1)} %bitcast.7), custom_call_target="tpu_custom_call" | custom-call | flops 3758096384 | bytes 22020096 | tf_op jit(solution)/shard_map/pallas_call | solution.py:304
  102.2 14.4 %shard_map.69 = (f32[896,7168]{1,0:T(8,128)}, f32[256,2048]{1,0:T(8,128)}) custom-call(bf16[896,512]{1,0:T(8,128)(2,1)} %get-tuple-element.8.turned_ref, bf16[512,7168]{1,0:T(8,128)(2,1)} %get-tuple-element.9.rows_ref, f32[8,128]{1,0:T(8,128)} %get-tuple-element.10.factor_ref, f32[256,2048]{1,0:T(8,128)} %get-tuple-element.11.down_in), custom_call_target="tpu_custom_call" | custom-call | flops 6576668672 | bytes 25690112 | tf_op jit(solution)/shard_map/pallas_call | solution.py:421

commit v7 on v6

--- a/solution.py
+++ b/solution.py
@@ -412,7 +412,7 @@
 def gram(turned, rows, factor, down):
     depth, width = rows.shape
     count = turned.shape[0]
-    tile = 512 if width % 512 == 0 else 128
+    tile = 1024 if width % 1024 == 0 else 128
     pieces = 2 if count % 16 == 0 else 1
     slots = 4
     vmem = pl.BlockSpec(memory_space=pltpu.VMEM)

time: 117 us -> 118 us (level)
  no operation moved by 1% of the time
where the time goes in v7:
time: 118 us; the launch traced here: 117 us
  Pallas kernels  117 us (99%)
    pallas_call x1, Pallas kernels, gather(): pl.pallas_call(functools.partial(gather_kernel, n, owners), out_shape=(ja...  102 us
    pallas_call x1, Pallas kernels, gram(): pl.pallas_call(functools.partial(gram_kernel, tile, pieces), out_shape=(j...  15.1 us

profile of v7, /device:TPU:0, one launch (start us, length us, event | category | flops | bytes accessed | tf_op | source)
XLA Modules:
  0.0 117.2 jit_solution(473606658835712681)
XLA Ops:
  0.6 101.5 %shard_map.68 = (bf16[512,7168]{1,0:T(8,128)(2,1)}, f32[256,2048]{1,0:T(8,128)}, f32[8,128]{1,0:T(8,128)}, bf16[896,512]{1,0:T(8,128)(2,1)}) custom-call(s32[8,256]{1,0:T(8,128)} %bitcast.8, s32[8,256]{1,0:T(8,128)} %bitcast.9, bf16[256,7168]{1,0:T(8,128)(2,1)} %tok_ref.1, bf16[256,7168]{1,0:T(8,128)(2,1)} %bitcast.6, bf16[256,7168]{1,0:T(8,128)(2,1)} %bitcast.7), custom_call_target="tpu_custom_call" | custom-call | flops 3758096384 | bytes 22020096 | tf_op jit(solution)/shard_map/pallas_call | solution.py:304
  102.2 15.1 %shard_map.69 = (f32[896,7168]{1,0:T(8,128)}, f32[256,2048]{1,0:T(8,128)}) custom-call(bf16[896,512]{1,0:T(8,128)(2,1)} %get-tuple-element.8.turned_ref, bf16[512,7168]{1,0:T(8,128)(2,1)} %get-tuple-element.9.rows_ref, f32[8,128]{1,0:T(8,128)} %get-tuple-element.10.factor_ref, f32[256,2048]{1,0:T(8,128)} %get-tuple-element.11.down_in), custom_call_target="tpu_custom_call" | custom-call | flops 6576668672 | bytes 25690112 | tf_op jit(solution)/shard_map/pallas_call | solution.py:421
